TPU v7x, 512 devices: a whole 4x8x8 slice. The times are simulated.
512 devices in a mesh: dp: 32 (over z, x), seq: 16 (over y, core).
Axes of the slice: x: 4, y: 8, z: 8, core: 2. Of those that a mesh axis runs over, the one named last changes fastest.
Arguments:
- features: bfloat16 [32, 3584, 1024], P('dp', 'seq'), may hold values from -6 to 6
- queries: bfloat16 [32, 3584, 1024], P('dp', 'seq'), may hold values from -4.5 to 4.5
- key_rows: bfloat16 [32, 3584, 1024], P('dp', 'seq'), may hold values from -4.5 to 4.5
- kernel: float32 [9, 1024], replicated, may hold values from -1.5 to 1.5
- out_weight: bfloat16 [1024, 1024], P(None, 'seq'), may hold values from -0.1875 to 0.1875
- cotangent: bfloat16 [32, 3584, 1024], P('dp', 'seq'), may hold values from -6 to 6
- lengths: int32 [32, 16], P('dp'), may hold values from 1 to 672, 3584 in all within a row
Outputs:
- layer_out: bfloat16 [32, 3584, 1024], P('dp', 'seq')
- grad_queries: bfloat16 [32, 3584, 1024], P('dp', 'seq')
- grad_keys: bfloat16 [32, 3584, 1024], P('dp', 'seq')
- grad_features: bfloat16 [32, 3584, 1024], P('dp', 'seq')
- grad_kernel: float32 [9, 1024], replicated
- grad_out_weight: float32 [1024, 1024], P(('dp', 'seq'))
Inputs may be any that keep to these rules, and one draw needn't show every extreme that they name: Each row holds 16 utterance lengths that sum to 3584.
All inputs are finite; a program needn't handle non-finite values.
Results may differ from a plain program's by a relative error of at most 0.012.
The roundings to bfloat16 on the way count: a program that leaves them out, or rounds other values in their place, can miss the bound.
Values may be sent and summed in bfloat16 or wider, within the bound.
A program may use at most 128 MiB of HBM per device.

v0:
```python
import jax
import jax.numpy as jnp
from jax import lax
from jax.sharding import PartitionSpec as P

HEADS = 8
HALF = 128


def with_halo(cells, sides, width):
    for axis, dim in sides:
        count = lax.axis_size(axis)
        ends = count - 1
        head = lax.slice_in_dim(cells, 0, width, axis=dim)
        tail = lax.slice_in_dim(cells, cells.shape[dim] - width, cells.shape[dim], axis=dim)
        cells = jnp.concatenate(
            [
                lax.ppermute(tail, axis, [(i, (i + 1) % count) for i in range(ends)]),
                cells,
                lax.ppermute(head, axis, [((i + 1) % count, i) for i in range(ends)]),
            ],
            axis=dim,
        )
    return cells


def from_behind(value, axis, steps):
    count = lax.axis_size(axis)
    leading, last = (max(0, -steps), min(count, count - steps))
    return lax.ppermute(value, axis, [(source, source + steps) for source in range(leading, last)])


def segment_of(positions, bounds):
    return jnp.sum((positions[:, None] >= bounds[None, :]).astype(jnp.int32), axis=1)


def pair_mask(center_pos, source_pos, bounds, seqlen):
    valid_c = (center_pos >= 0) & (center_pos < seqlen)
    valid_s = (source_pos >= 0) & (source_pos < seqlen)
    return valid_c & valid_s & (segment_of(center_pos, bounds) == segment_of(source_pos, bounds))


def window_mask(query_pos, key_pos, bounds, seqlen):
    valid_q = (query_pos >= 0) & (query_pos < seqlen)
    valid_k = (key_pos >= 0) & (key_pos < seqlen)
    same = segment_of(query_pos, bounds)[:, None] == segment_of(key_pos, bounds)[None, :]
    near = jnp.abs(query_pos[:, None] - key_pos[None, :]) <= HALF
    return valid_q[:, None] & valid_k[None, :] & same & near


def depthwise(source, source_pos, kernel, row_count, bounds, seqlen):
    reach = (kernel.shape[0] - 1) // 2
    center = source_pos[reach : reach + row_count]
    running = jnp.zeros((row_count, source.shape[1]), jnp.float32)
    for tap_index in range(kernel.shape[0]):
        matches = pair_mask(center, source_pos[tap_index : tap_index + row_count], bounds, seqlen)
        term = kernel[tap_index][None, :] * source[tap_index : tap_index + row_count].astype(
            jnp.float32
        )
        running = running + jnp.where(matches[:, None], term, 0.0)
    return running


def conv_back(grad_rim, rim_pos, kernel, row_count, bounds, seqlen):
    reach = (kernel.shape[0] - 1) // 2
    center = rim_pos[reach : reach + row_count]
    running = jnp.zeros((row_count, grad_rim.shape[1]), jnp.float32)
    for tap_index in range(kernel.shape[0]):
        low = 2 * reach - tap_index
        matches = pair_mask(center, rim_pos[low : low + row_count], bounds, seqlen)
        term = kernel[tap_index][None, :] * grad_rim[low : low + row_count]
        running = running + jnp.where(matches[:, None], term, 0.0)
    return running


def kernel_terms(grad_values, input_rim, rim_pos, kernel, row_count, bounds, seqlen):
    reach = (kernel.shape[0] - 1) // 2
    center = rim_pos[reach : reach + row_count]
    rows_out = []
    for tap_index in range(kernel.shape[0]):
        matches = pair_mask(center, rim_pos[tap_index : tap_index + row_count], bounds, seqlen)
        term = grad_values * input_rim[tap_index : tap_index + row_count].astype(jnp.float32)
        rows_out.append(jnp.sum(jnp.where(matches[:, None], term, 0.0), axis=0))
    return jnp.stack(rows_out)


def head_inner(back, mixed):
    product = back.astype(jnp.float32) * mixed.astype(jnp.float32)
    return jnp.sum(product.reshape(product.shape[0], HEADS, -1), axis=2).T


def forward_attention(query_block, key_ext, value_ext, allowed):
    row_count = query_block.shape[0]
    query_h = query_block.reshape(row_count, HEADS, -1)
    key_h = key_ext.reshape(key_ext.shape[0], HEADS, -1)
    value_h = value_ext.reshape(value_ext.shape[0], HEADS, -1)
    score_scale = query_h.shape[-1] ** (-0.5)
    scores = (
        jnp.einsum("thd,uhd->htu", query_h, key_h, preferred_element_type=jnp.float32) * score_scale
    )
    masked = jnp.where(allowed[None], scores, -jnp.inf)
    row_max = jnp.max(masked, axis=-1, keepdims=True)
    exponent = jnp.where(allowed[None], jnp.exp(masked - row_max), 0.0)
    sums = jnp.sum(exponent, axis=-1, keepdims=True)
    probs_bf = (exponent / sums).astype(jnp.bfloat16)
    mixed = jnp.einsum("htu,uhd->thd", probs_bf, value_h, preferred_element_type=jnp.float32)
    log_total = (row_max + jnp.log(sums))[..., 0]
    return (mixed.reshape(row_count, -1).astype(jnp.bfloat16), log_total)


def backward_attention(query_block, key_ext, value_ext, back_block, inner, log_total, allowed):
    row_count = query_block.shape[0]
    query_h = query_block.reshape(row_count, HEADS, -1)
    back_h = back_block.reshape(row_count, HEADS, -1)
    key_h = key_ext.reshape(key_ext.shape[0], HEADS, -1)
    value_h = value_ext.reshape(value_ext.shape[0], HEADS, -1)
    score_scale = query_h.shape[-1] ** (-0.5)
    scores = (
        jnp.einsum("thd,uhd->htu", query_h, key_h, preferred_element_type=jnp.float32) * score_scale
    )
    again = jnp.where(
        allowed[None], jnp.exp(jnp.where(allowed[None], scores, 0.0) - log_total[..., None]), 0.0
    )
    dprob = jnp.einsum("thd,uhd->htu", back_h, value_h, preferred_element_type=jnp.float32)
    dscore = (again * (dprob - inner[..., None])).astype(jnp.bfloat16)
    grad_q = None
    grad_k = None
    grad_v = None
    grad_q = (
        jnp.einsum("htu,uhd->thd", dscore, key_h, preferred_element_type=jnp.float32).reshape(
            row_count, -1
        )
        * score_scale
    )
    again_bf = again.astype(jnp.bfloat16)
    grad_k = (
        jnp.einsum("htu,thd->uhd", dscore, query_h, preferred_element_type=jnp.float32).reshape(
            key_ext.shape[0], -1
        )
        * score_scale
    )
    grad_v = jnp.einsum(
        "htu,thd->uhd", again_bf, back_h, preferred_element_type=jnp.float32
    ).reshape(key_ext.shape[0], -1)
    return (grad_q, grad_k, grad_v)


def body(features, queries, key_rows, kernel, out_weight, cotangent, lengths):
    inputs_row = features[0]
    query_row = queries[0]
    key_row = key_rows[0]
    cot_row = cotangent[0]
    frames, model_width = inputs_row.shape
    seq_count = lax.axis_size("seq")
    seqlen = frames * seq_count
    offset = lax.axis_index("seq") * frames
    bounds = jnp.cumsum(lengths[0])
    reach = (kernel.shape[0] - 1) // 2
    own_pos = offset + jnp.arange(frames, dtype=jnp.int32)
    ext_pos = offset - HALF + jnp.arange(frames + 2 * HALF, dtype=jnp.int32)
    rim_pos = offset - reach + jnp.arange(frames + 2 * reach, dtype=jnp.int32)
    input_rim = with_halo(inputs_row, (("seq", 0),), reach)
    own_values = depthwise(input_rim, rim_pos, kernel, frames, bounds, seqlen).astype(jnp.bfloat16)
    paired = with_halo(jnp.stack([key_row, own_values]), (("seq", 1),), HALF)
    key_ext = paired[0]
    value_ext = paired[1]
    allowed = window_mask(own_pos, ext_pos, bounds, seqlen)
    mixed, log_total = forward_attention(query_row, key_ext, value_ext, allowed)
    layer = jnp.dot(
        mixed,
        lax.all_gather(out_weight, "seq", axis=1, tiled=True),
        preferred_element_type=jnp.float32,
    )
    columns = cot_row
    back_sum = lax.dot_general(
        columns,
        lax.all_gather(out_weight, "seq", axis=1, tiled=True),
        (((1,), (1,)), ((), ())),
        preferred_element_type=jnp.float32,
    )
    back = back_sum.astype(jnp.bfloat16)
    norm = float(lax.axis_size("dp") * seqlen) ** (-0.5)
    columns = mixed
    grad_weight = (
        lax.psum_scatter(
            lax.dot_general(
                columns, cot_row, (((0,), (0,)), ((), ())), preferred_element_type=jnp.float32
            ),
            ("dp", "seq"),
            scatter_dimension=0,
            tiled=True,
        )
        * norm
    )
    inner = head_inner(back, mixed)
    grad_q, grad_k_ext, grad_v_ext = backward_attention(
        query_row, key_ext, value_ext, back, inner, log_total, allowed
    )
    stacked = jnp.stack([grad_k_ext, grad_v_ext])
    from_right = from_behind(stacked[:, :HALF].astype(jnp.bfloat16), "seq", -1).astype(jnp.float32)
    from_left = from_behind(stacked[:, frames + HALF :].astype(jnp.bfloat16), "seq", 1).astype(
        jnp.float32
    )
    own_rows = stacked[:, HALF : HALF + frames]
    own_rows = own_rows + jnp.pad(from_left, ((0, 0), (0, frames - HALF), (0, 0)))
    own_rows = own_rows + jnp.pad(from_right, ((0, 0), (frames - HALF, 0), (0, 0)))
    grad_k = own_rows[0]
    grad_values = own_rows[1]
    grad_rim = with_halo(grad_values, (("seq", 0),), reach)
    grad_in = conv_back(grad_rim, rim_pos, kernel, frames, bounds, seqlen)
    kernel_part = kernel_terms(grad_values, input_rim, rim_pos, kernel, frames, bounds, seqlen)
    grad_kernel = lax.psum(kernel_part, ("dp", "seq")) * norm
    return (
        layer.astype(jnp.bfloat16)[None],
        grad_q.astype(jnp.bfloat16)[None],
        grad_k.astype(jnp.bfloat16)[None],
        grad_in.astype(jnp.bfloat16)[None],
        grad_kernel,
        grad_weight,
    )


def solution(mesh):
    in_specs = (
        P("dp", "seq", None),
        P("dp", "seq", None),
        P("dp", "seq", None),
        P(),
        P(None, "seq"),
        P("dp", "seq", None),
        P("dp", None),
    )
    out_specs = (
        P("dp", "seq", None),
        P("dp", "seq", None),
        P("dp", "seq", None),
        P("dp", "seq", None),
        P(),
        P(("dp", "seq"), None),
    )
    return jax.shard_map(body, mesh=mesh, in_specs=in_specs, out_specs=out_specs, check_vma=False)
```

profile of v0, /device:TPU:1, one launch (start us, length us, event | category | flops | bytes accessed | tf_op | source)
XLA Modules:
  0.0 502.0 jit_solution(1159452565191691560)
XLA Ops:
  8.9 4.6 collective-permute-start
  13.5 5.5 %collective-permute-start.1 = (bf16[4,1024]{1,0:T(4,128)(2,1)S(1)}, bf16[4,1024]{1,0:T(4,128)(2,1)S(1)}, u32[]{:S(2)}, u32[]{:S(2)}) collective-permute-start(bf16[4,1024]{1,0:T(4,128)(2,1)S(1)} %get-tuple-element.36), channel_id=1, source_target_pairs={{1,0},{2,1},{3,2},{4,3},{5,4},{6,5},{7,6},{8,7},{9,8},{10,9},{11,1... | collective-permute-start | bytes 24584 | tf_op jit(solution)/shard_map/ppermute | solution.py:20
  22.5 6.1 %fusion.109 = bf16[1,224,1024]{2,1,0:T(8,128)(2,1)S(1)} fusion(bf16[4,1024]{1,0:T(4,128)(2,1)S(1)} %collective-permute-done.1, bf16[224,1024]{1,0:T(8,128)(2,1)} %bitcast.135, f32[1024]{0:T(1024)S(1)} %bitcast.161, pred[224]{0:T(512)(128)(4,1)S(1)} %get-tuple-element.47, f32[1024]{0:T(1024)S(1)} %bitcast.163, pred[224]{0:T(512)(128)(4,1)S(1)} %get-tuple-element.48, ...), kind=kLoop, calls=%fused_computation.162 | loop fusion | flops 13762560 | bytes 972768 | tf_op jit(solution)/shard_map/stack | solution.py:164
  28.6 1.1 fusion.94
  29.7 1.9 collective-permute-start.2
  31.7 2.4 collective-permute-start.3
  34.5 3.3 collective-permute-done.2
  37.8 4.4 collective-permute-done.3
  45.0 1.2 fusion.4
  46.2 1.8 fusion.20
  48.0 2.7 fusion.101
  51.4 290.0 %all-reduce.5.cloned.1.call-done = f32[1024,1024]{1,0:T(8,128)} async-done(((f32[1024,1024]{1,0:T(8,128)}), f32[1024,1024]{1,0:T(8,128)}) %all-reduce.5.cloned.1.call-update) | async-done | bytes 4194320
  341.4 1.4 dynamic-slice_multiply_fusion
  342.8 2.2 convolution_convert_fusion
  345.7 5.1 %fusion.14 = f32[480,8,128]{2,0,1:T(8,128)} fusion(f32[8,480,224]{1,2,0:T(8,128)} %copy-done.4, f32[8,224]{1,0:T(8,128)S(1)} %log_add_fusion, pred[224,480]{1,0:T(8,128)(4,1)S(1)} %fusion.108, bf16[224,1024]{1,0:T(8,128)(2,1)S(1)} %convolution_convert_fusion), kind=kOutput, calls=%fused_computation.27 | convolution fusion | flops 224501760 | bytes 5980160 | tf_op jit(solution)/shard_map/htu,thd->uhd/dot_general | solution.py:142
  350.8 1.6 multiply_convert_fusion
  353.6 2.4 copy.56
  356.1 1.7 mul.270
  357.7 4.0 copy.58
  361.7 2.7 stack_reshape.3
  364.5 1.4 copy-done.2
  366.5 1.6 copy-done.1
  368.0 2.7 collective-permute-start.4
  370.7 1.9 collective-permute-start.5
  374.5 3.2 fusion.21
  378.4 2.9 collective-permute-done.5
  381.3 2.0 fusion.8
  384.4 1.6 fusion.57
  386.1 98.7 %psum.7 = f32[9,1024]{1,0:T(8,128)S(1)} all-reduce(f32[9,1024]{1,0:T(8,128)S(1)} %stack.52), channel_id=1, replica_groups=mesh['dp'=32,'seq'=16] {'dp','seq'}, use_global_device_ids=true, to_apply=%region_24.25 | all-reduce | flops 9216 | bytes 73728 | tf_op jit(solution)/shard_map/psum | solution.py:212
  484.7 2.6 collective-permute-start.6
  487.3 2.9 collective-permute-start.7
  491.8 2.8 fusion.110
  (77 shorter events, 15.8 us)
Async XLA Ops:
  8.0 40.0 %copy-start = (bf16[1,224,1024]{2,1,0:T(8,128)(2,1)S(1)}, bf16[1,224,1024]{2,1,0:T(8,128)(2,1)}, u32[]{:S(2)}) copy-start(bf16[1,224,1024]{2,1,0:T(8,128)(2,1)} %param.12) | copy-start | bytes 1376260
  8.0 34.1 %copy-start.8 = (bf16[1,224,1024]{2,1,0:T(8,128)(2,1)S(1)}, bf16[1,224,1024]{2,1,0:T(8,128)(2,1)}, u32[]{:S(2)}) copy-start(bf16[1,224,1024]{2,1,0:T(8,128)(2,1)} %param.9) | copy-start | bytes 1376260
  8.0 333.4 %all-reduce.5.cloned.1.call-start = ((), (), s32[]{:S(2)}) async-start(), calls=%async_computation.1 | async-start | bytes 8388608
  8.9 13.6 %collective-permute-start = (bf16[4,1024]{1,0:T(4,128)(2,1)S(1)}, bf16[4,1024]{1,0:T(4,128)(2,1)S(1)}, u32[]{:S(2)}, u32[]{:S(2)}) collective-permute-start(bf16[4,1024]{1,0:T(4,128)(2,1)S(1)} %get-tuple-element.35), channel_id=1, source_target_pairs={{0,1},{1,2},{2,3},{3,4},{4,5},{5,6},{6,7},{7,8},{8,9},{9,10},{10,1... | collective-permute-start | bytes 24584 | tf_op jit(solution)/shard_map/ppermute | solution.py:18
  13.5 9.0 %collective-permute-start.1 = (bf16[4,1024]{1,0:T(4,128)(2,1)S(1)}, bf16[4,1024]{1,0:T(4,128)(2,1)S(1)}, u32[]{:S(2)}, u32[]{:S(2)}) collective-permute-start(bf16[4,1024]{1,0:T(4,128)(2,1)S(1)} %get-tuple-element.36), channel_id=1, source_target_pairs={{1,0},{2,1},{3,2},{4,3},{5,4},{6,5},{7,6},{8,7},{9,8},{10,9},{11,1... | collective-permute-start | bytes 24584 | tf_op jit(solution)/shard_map/ppermute | solution.py:20
  29.7 8.0 %collective-permute-start.2 = (bf16[2,128,1024]{2,1,0:T(8,128)(2,1)S(1)}, bf16[2,128,1024]{2,1,0:T(8,128)(2,1)S(1)}, u32[]{:S(2)}, u32[]{:S(2)}) collective-permute-start(bf16[2,128,1024]{2,1,0:T(8,128)(2,1)S(1)} %get-tuple-element.33), channel_id=1, source_target_pairs={{0,1},{1,2},{2,3},{3,4},{4,5},{5,6},{6,7},{7,8},{8,9},{9,10},{10,1... | collective-permute-start | bytes 1572872 | tf_op jit(solution)/shard_map/ppermute | solution.py:18
  31.7 10.5 %collective-permute-start.3 = (bf16[2,128,1024]{2,1,0:T(8,128)(2,1)S(1)}, bf16[2,128,1024]{2,1,0:T(8,128)(2,1)S(1)}, u32[]{:S(2)}, u32[]{:S(2)}) collective-permute-start(bf16[2,128,1024]{2,1,0:T(8,128)(2,1)S(1)} %get-tuple-element.34), channel_id=1, source_target_pairs={{1,0},{2,1},{3,2},{4,3},{5,4},{6,5},{7,6},{8,7},{9,8},{10,9},{11,1... | collective-permute-start | bytes 1572872 | tf_op jit(solution)/shard_map/ppermute | solution.py:20
  42.8 3.5 copy-start.11
  43.0 1.0 copy-start.9
  45.0 3.0 copy-start.4
  50.8 292.0 %all-gather.2.cloned.1.call-start = ((), (), s32[]{:S(2)}) async-start(), calls=%async_computation | async-start | bytes 2228224 | tf_op jit(solution)/shard_map/all_gather | solution.py:171
  345.7 5.1 %copy-start.5 = (f32[8,480,224]{1,2,0:T(8,128)S(1)}, f32[8,480,224]{1,2,0:T(8,128)}, u32[]{:S(2)}) copy-start(f32[8,480,224]{1,2,0:T(8,128)} %copy-done.4) | copy-start | bytes 10321924
  345.7 5.1 %copy-start.12 = (bf16[60,8,8,128]{3,2,1,0:T(8,128)(2,1)S(1)}, bf16[60,8,8,128]{3,2,1,0:T(8,128)(2,1)}, u32[]{:S(2)}) copy-start(bf16[60,8,8,128]{3,2,1,0:T(8,128)(2,1)} %copy-done.11) | copy-start | bytes 2949124
  352.4 1.3 copy-start.6
  364.4 1.5 copy-start.2
  366.0 2.0 copy-start.1
  366.1 6.6 %copy-start.7 = (bf16[8,224,480]{2,1,0:T(8,128)(2,1)S(1)}, bf16[8,224,480]{2,1,0:T(8,128)(2,1)}, u32[]{:S(2)}) copy-start(bf16[8,224,480]{2,1,0:T(8,128)(2,1)} %copy-done.6) | copy-start | bytes 5160964
  366.1 6.6 %copy-start.10 = (bf16[60,8,8,128]{3,2,1,0:T(8,128)(2,1)S(1)}, bf16[60,8,8,128]{3,2,1,0:T(8,128)(2,1)}, u32[]{:S(2)}) copy-start(bf16[60,8,8,128]{3,2,1,0:T(8,128)(2,1)} %copy-done.9) | copy-start | bytes 2949124
  368.0 9.6 %collective-permute-start.4 = (bf16[2,128,1024]{2,1,0:T(8,128)(2,1)S(1)}, bf16[2,128,1024]{2,1,0:T(8,128)(2,1)S(1)}, u32[]{:S(2)}, u32[]{:S(2)}) collective-permute-start(bf16[2,128,1024]{2,1,0:T(8,128)(2,1)S(1)} %get-tuple-element.27), channel_id=1, source_target_pairs={{0,1},{1,2},{2,3},{3,4},{4,5},{5,6},{6,7},{7,8},{8,9},{9,10},{10,1... | collective-permute-start | bytes 1572872 | tf_op jit(solution)/shard_map/ppermute | solution.py:30
  370.7 10.6 %collective-permute-start.5 = (bf16[2,128,1024]{2,1,0:T(8,128)(2,1)S(1)}, bf16[2,128,1024]{2,1,0:T(8,128)(2,1)}, u32[]{:S(2)}, u32[]{:S(2)}) collective-permute-start(bf16[2,128,1024]{2,1,0:T(8,128)(2,1)S(1)} %get-tuple-element.28), channel_id=1, source_target_pairs={{1,0},{2,1},{3,2},{4,3},{5,4},{6,5},{7,6},{8,7},{9,8},{10,9},{11,1... | collective-permute-start | bytes 1572872 | tf_op jit(solution)/shard_map/ppermute | solution.py:30
  377.6 5.8 %copy-start.3 = (bf16[1,224,1024]{2,1,0:T(8,128)(2,1)S(1)}, bf16[1,224,1024]{2,1,0:T(8,128)(2,1)}, u32[]{:S(2)}) copy-start(bf16[1,224,1024]{2,1,0:T(8,128)(2,1)} %param.7) | copy-start | bytes 1376260
  377.7 0.8 copy-start.13
  484.7 7.0 %collective-permute-start.6 = (f32[4,1024]{1,0:T(4,128)S(1)}, f32[4,1024]{1,0:T(4,128)S(1)}, u32[]{:S(2)}, u32[]{:S(2)}) collective-permute-start(f32[4,1024]{1,0:T(4,128)S(1)} %get-tuple-element.31), channel_id=1, source_target_pairs={{1,0},{2,1},{3,2},{4,3},{5,4},{6,5},{7,6},{8,7},{9,8},{10,9},{11,1... | collective-permute-start | bytes 49160 | tf_op jit(solution)/shard_map/ppermute | solution.py:20
  487.3 4.4 collective-permute-start.7
Sparse Core Ops, SparseCore 0:
  50.9 290.4 all-reduce.4
Sparse Core Ops, SparseCore 1:
  53.4 46.4 all-gather.1
where the time goes:
time: 503 us; the launch traced here: 502 us
  waiting for transfers between devices  301 us (60%)
  blocking collectives  98.7 us (20%)
  starting transfers between devices  24.8 us (5%)
  local copies, waits for them, and re-layouts  23.2 us (5%)
  other arithmetic  19.5 us (4%)
  matrix products  19 us (4%)
  between operations  16 us (3%)
    unnamed x3, waiting for transfers between devices  290 us
    psum x1, blocking collectives, body(): grad_kernel = lax.psum(kernel_part, ('dp', 'seq')) * norm  98.7 us
    ppermute x3, starting transfers between devices, with_halo(): lax.ppermute(head, axis, [((i + 1) % count, i) for i in range(ends)])  10.5 us
  transfers between devices with their start and end apart: 10, of which 4 were waited for; matrix products, arithmetic and copies ran while one was open for 2% of the time, Pallas kernels for 0%

commit v1 on v0

v1 whole, which is shorter than its diff:
```python
import functools
import math

import jax
import jax.numpy as jnp
from jax import lax
from jax.experimental import pallas as pl
from jax.experimental.pallas import tpu as pltpu
from jax.sharding import PartitionSpec as P

MESH = pl.DeviceIdType.MESH
F32 = jnp.float32
BF16 = jnp.bfloat16

HALF = 128
TAPS = 9
REACH = 4
RIM = 16
UTT = 16
ROWS = 224
WIDTH = 1024
HEAD = 128
PAIR = 256
GROUPS = 4
NX = 4
NZ = 8
NY = 8
EXT = ROWS + 2 * HALF
FEXT = EXT + 2 * RIM
FHALO = HALF + RIM
BLK = 112
SPAN = 384
BLKOFF = 96
NSEM = 160


def dot(a, b, contract):
    return lax.dot_general(a, b, ((contract[:1], contract[1:]), ((), ())), preferred_element_type=F32)


def kernel(
    norm,
    feat, qry, key, ker, wgt, cot, lens,
    o_layer, o_gq, o_gk, o_gf, o_gker, o_gw,
    fext, fs, kext, qv, cotv, kerv, segs, taps, bias, vext, probs, mixed,
    wown, wsib, wpiece, wblk, wfull,
    gsend, gown, gcore, gx, gxr, gz, gzr, gs, gsr, gwv,
    dqv, dkx, dvx, dks, dvs, dkr, dvr, dkv, gfv, lay,
    kp, kpr, kz, kzr, ky, kyr, kfin, kall, kout,
    ss, rs, ls,
):
    dp = lax.axis_index("dp")
    sq = lax.axis_index("seq")
    z, x = dp // NX, dp % NX
    y, c = sq // 2, sq % 2
    e = 2 * x + c
    nseq = 2 * NY
    seqlen = nseq * ROWS
    offset = sq * ROWS

    def dev(d, s):
        return {"dp": d, "seq": s}

    sib = dev(dp, sq + 1 - 2 * c)
    right = dev(dp, (sq + 1) % nseq)
    left = dev(dp, (sq + nseq - 1) % nseq)

    def seq_peer(k):
        return dev(dp, (sq + k) % nseq)

    def y_peer(k):
        return dev(dp, ((y + k) % NY) * 2 + c)

    def z_peer(k):
        return dev(((z + k) % NZ) * NX + x, sq)

    def x_peer(k):
        return dev(z * NX + (x + k) % NX, sq)

    def xc_peer(k):
        other = (e + k) % 8
        return dev(z * NX + other // 2, y * 2 + other % 2)

    barrier = pltpu.get_barrier_semaphore()
    greeted = 0
    for k in range(1, nseq):
        pl.semaphore_signal(barrier, inc=1, device_id=seq_peer(k), device_id_type=MESH)
        greeted += 1
    for k in range(1, NZ):
        pl.semaphore_signal(barrier, inc=1, device_id=z_peer(k), device_id_type=MESH)
        greeted += 1
    for k in range(1, 8):
        pl.semaphore_signal(barrier, inc=1, device_id=xc_peer(k), device_id_type=MESH)
        greeted += 1

    used = [0, 0]
    sends = []

    def remote(src, dst, device):
        index = used[0]
        used[0] += 1
        copy = pltpu.make_async_remote_copy(
            src_ref=src, dst_ref=dst, send_sem=ss.at[index], recv_sem=rs.at[index],
            device_id=device, device_id_type=MESH,
        )
        copy.start()
        sends.append(copy)
        return copy

    def local(src, dst):
        index = used[1]
        used[1] += 1
        copy = pltpu.make_async_copy(src, dst, ls.at[index])
        copy.start()
        return copy

    def cols(g):
        return pl.ds(pl.multiple_of(g * PAIR, PAIR), PAIR)

    wrow = pl.multiple_of(e * HEAD + 16 * z, 16)
    srow = pl.multiple_of((2 * x + 1 - c) * HEAD + 16 * z, 16)
    wown_in = local(wgt.at[pl.ds(wrow, 16), :], wown)
    loads = []
    for g in range(GROUPS):
        loads.append([
            local(feat.at[:, cols(g)], fext.at[g, pl.ds(FHALO, ROWS)]),
            local(key.at[:, cols(g)], kext.at[g, pl.ds(HALF, ROWS)]),
            local(qry.at[:, cols(g)], qv.at[g]),
        ])
    ker_in = local(ker, kerv)
    cot_in = local(cot, cotv)

    pl.semaphore_wait(barrier, greeted)

    w_core = remote(wgt.at[pl.ds(srow, 16), :], wsib, sib)
    halos = []
    for g in range(GROUPS):
        halos.append([
            remote(feat.at[pl.ds(ROWS - FHALO, FHALO), cols(g)], fext.at[g, pl.ds(0, FHALO)], right),
            remote(feat.at[pl.ds(0, FHALO), cols(g)], fext.at[g, pl.ds(FHALO + ROWS, FHALO)], left),
            remote(key.at[pl.ds(ROWS - HALF, HALF), cols(g)], kext.at[g, pl.ds(0, HALF)], right),
            remote(key.at[pl.ds(0, HALF), cols(g)], kext.at[g, pl.ds(HALF + ROWS, HALF)], left),
        ])

    bounds = []
    total = lens[0, 0]
    bounds.append(total)
    for k in range(1, UTT):
        total = total + lens[0, k]
        bounds.append(total)

    def segment(pos):
        seg = jnp.where(pos < 0, -1, 0)
        for bound in bounds:
            seg = seg + jnp.where(pos >= bound, 1, 0)
        return seg

    for r in range(0, FEXT, 64):
        pos = offset - FHALO + r + lax.broadcasted_iota(jnp.int32, (64, HEAD), 0)
        segs[pl.ds(r, 64), :] = segment(pos)
    for r in range(0, EXT, 96):
        center = segs[pl.ds(RIM + r, 96), :]
        for j in range(TAPS):
            near = segs[pl.ds(RIM - REACH + j + r, 96), :]
            taps[j, pl.ds(r, 96), :] = jnp.where(center == near, 1.0, 0.0).astype(F32)
    for b in range(2):
        colpos = offset - HALF + BLKOFF * b + lax.broadcasted_iota(jnp.int32, (8, SPAN), 1)
        seg_col = segment(colpos)[0:1, :]
        seg_row = segs[pl.ds(FHALO + BLK * b, BLK), :]
        seg_row = jnp.concatenate([seg_row] * (SPAN // HEAD), axis=1)
        gap = (
            lax.broadcasted_iota(jnp.int32, (BLK, SPAN), 0) + (BLK * b + HALF - BLKOFF * b)
            - lax.broadcasted_iota(jnp.int32, (BLK, SPAN), 1)
        )
        ok = (seg_row == seg_col) & (gap <= HALF) & (gap >= -HALF)
        bias[b] = jnp.where(ok, 0.0, -jnp.inf).astype(F32)

    wown_in.wait()
    w_core.wait_recv()
    mine = wown[...].astype(F32)
    theirs = wsib[...].astype(F32)
    first = jnp.concatenate([mine, theirs], axis=1)
    second = jnp.concatenate([theirs, mine], axis=1)
    piece = jnp.where(c == 0, first, second).astype(BF16)
    wpiece[...] = piece
    ycol = pl.ds(pl.multiple_of(y * HEAD, HEAD), HEAD)
    wblk[:, ycol] = piece
    w_y = [remote(wpiece, wblk.at[:, ycol], y_peer(k)) for k in range(1, NY)]

    scale = HEAD ** -0.5
    scale2 = scale * math.log2(math.e)

    def forward(g):
        for copy in loads[g]:
            copy.wait()
        for copy in halos[g]:
            copy.wait_recv()
        for j in range(2):
            lanes = pl.ds(j * HEAD, HEAD)
            h = 2 * g + j
            fs[h] = fext[g, :, lanes].astype(F32)
            kw = kerv[:, pl.ds(h * HEAD, HEAD)]
            for r in range(0, EXT, 96):
                acc = kw[REACH:REACH + 1, :] * fs[h, pl.ds(r + RIM, 96), :]
                for t in range(TAPS):
                    if t != REACH:
                        f = fs[h, pl.ds(r + RIM - REACH + t, 96), :]
                        acc = acc + (f * taps[t, pl.ds(r, 96), :]) * kw[t:t + 1, :]
                vext[g, pl.ds(r, 96), lanes] = acc.astype(BF16)
        for j in range(2):
            lanes = pl.ds(j * HEAD, HEAD)
            h = 2 * g + j
            for b in range(2):
                qb = qv[g, pl.ds(BLK * b, BLK), lanes]
                kb = kext[g, pl.ds(BLKOFF * b, SPAN), lanes]
                s = dot(qb, kb, (1, 1)) * scale2 + bias[b]
                top = jnp.max(s, axis=1, keepdims=True)
                ex = jnp.exp2(s - top)
                p = ex * (1.0 / jnp.sum(ex, axis=1, keepdims=True))
                probs[h, b] = p
                vb = vext[g, pl.ds(BLKOFF * b, SPAN), lanes]
                mixed[pl.ds(BLK * b, BLK), pl.ds(h * HEAD, HEAD)] = dot(p.astype(BF16), vb, (1, 0)).astype(BF16)

    ker_in.wait()
    forward(0)

    for copy in w_y:
        copy.wait_recv()
    own_rows = pl.ds(wrow, 16)
    wfull[own_rows, :] = wblk[...]
    w_z = [remote(wblk, wfull.at[own_rows, :], z_peer(k)) for k in range(1, NZ)]

    forward(1)

    for copy in w_z:
        copy.wait_recv()
    head_rows = pl.ds(pl.multiple_of(e * HEAD, HEAD), HEAD)
    w_s = [remote(wfull.at[head_rows, :], wfull.at[head_rows, :], sib)]
    w_x = {}
    for k in (1, 3, 2):
        w_x[k] = remote(wfull.at[head_rows, :], wfull.at[head_rows, :], x_peer(k))

    forward(2)
    forward(3)

    cot_in.wait()
    sib_cols = pl.ds(pl.multiple_of((1 - c) * 512, 512), 512)
    own_cols = pl.ds(pl.multiple_of(c * 512, 512), 512)
    for i in range(NZ):
        mb = mixed[:, pl.ds(i * HEAD, HEAD)]
        gsend[pl.ds(i * HEAD, HEAD), :] = dot(mb, cotv[:, sib_cols], (0, 0)).astype(BF16)
    g_core = remote(gsend, gcore, sib)
    for i in range(NZ):
        mb = mixed[:, pl.ds(i * HEAD, HEAD)]
        gown[pl.ds(i * HEAD, HEAD), :] = dot(mb, cotv[:, own_cols], (0, 0))

    def w_forward(k):
        w_x[k].wait_recv()
        rows = pl.ds(pl.multiple_of((2 * ((x + NX - k) % NX) + c) * HEAD, HEAD), HEAD)
        w_s.append(remote(wfull.at[rows, :], wfull.at[rows, :], sib))

    def backward(step, g):
        w_s[step].wait_recv()
        back = dot(cotv[...], wfull[pl.ds(pl.multiple_of(g * PAIR, PAIR), PAIR), :], (1, 1)).astype(BF16)
        for j in range(2):
            lanes = pl.ds(j * HEAD, HEAD)
            h = 2 * g + j
            bh = back[:, j * HEAD:(j + 1) * HEAD]
            mh = mixed[:, pl.ds(pl.multiple_of(h * HEAD, HEAD), HEAD)]
            inner = jnp.sum(bh.astype(F32) * mh.astype(F32), axis=1, keepdims=True)
            parts = []
            for b in range(2):
                rows = slice(BLK * b, BLK * b + BLK)
                p = probs[h, b]
                kb = kext[g, pl.ds(BLKOFF * b, SPAN), lanes]
                vb = vext[g, pl.ds(BLKOFF * b, SPAN), lanes]
                qb = qv[g, pl.ds(BLK * b, BLK), lanes]
                ds = (p * (dot(bh[rows], vb, (1, 1)) - inner[rows])).astype(BF16)
                dqv[g, pl.ds(BLK * b, BLK), lanes] = (dot(ds, kb, (1, 0)) * scale).astype(BF16)
                parts.append((dot(ds, qb, (0, 0)) * scale, dot(p.astype(BF16), bh[rows], (0, 0))))
            for out, first, second in ((dkx, parts[0][0], parts[1][0]), (dvx, parts[0][1], parts[1][1])):
                out[h, pl.ds(0, BLKOFF), :] = first[:BLKOFF]
                out[h, pl.ds(BLKOFF, SPAN - BLKOFF), :] = first[BLKOFF:] + second[:SPAN - BLKOFF]
                out[h, pl.ds(SPAN, EXT - SPAN), :] = second[SPAN - BLKOFF:]
            dks[step, 0, :, lanes] = dkx[h, pl.ds(0, HALF), :].astype(BF16)
            dks[step, 1, :, lanes] = dkx[h, pl.ds(EXT - HALF, HALF), :].astype(BF16)
            dvs[step, 0, :, lanes] = dvx[h, pl.ds(0, FHALO), :].astype(BF16)
            dvs[step, 1, :, lanes] = dvx[h, pl.ds(EXT - FHALO, FHALO), :].astype(BF16)
        copies = [
            remote(dvs.at[step, 0], dvr.at[step, 0], left),
            remote(dvs.at[step, 1], dvr.at[step, 1], right),
            remote(dks.at[step, 0], dkr.at[step, 0], left),
            remote(dks.at[step, 1], dkr.at[step, 1], right),
        ]
        out = local(dqv.at[g], o_gq.at[:, cols(g)])
        for j in range(2):
            h = 2 * g + j
            sums = [jnp.zeros((8, HEAD), F32) for _ in range(TAPS)]
            for r in range(0, EXT, 96):
                gv = dvx[h, pl.ds(r, 96), :]
                for t in range(TAPS):
                    term = gv * fs[h, pl.ds(r + RIM - REACH + t, 96), :]
                    if t != REACH:
                        term = term * taps[t, pl.ds(r, 96), :]
                    sums[t] = sums[t] + jnp.sum(term.reshape(12, 8, HEAD), axis=0)
            rows = [jnp.sum(v, axis=0, keepdims=True) for v in sums]
            rows.append(jnp.zeros((16 - TAPS, HEAD), F32))
            kp[h] = jnp.concatenate(rows, axis=0)
        return copies, out

    def finish(step, g, copies):
        for copy in copies:
            copy.wait_recv()
        for j in range(2):
            lanes = pl.ds(j * HEAD, HEAD)
            h = 2 * g + j
            dkx[h, pl.ds(HALF, HALF), :] += dkr[step, 1, :, lanes].astype(F32)
            dkx[h, pl.ds(ROWS, HALF), :] += dkr[step, 0, :, lanes].astype(F32)
            dkv[g, :, lanes] = dkx[h, pl.ds(HALF, ROWS), :].astype(BF16)
            dvx[h, pl.ds(HALF - RIM, FHALO), :] += dvr[step, 1, :, lanes].astype(F32)
            dvx[h, pl.ds(ROWS, FHALO), :] += dvr[step, 0, :, lanes].astype(F32)
            kw = kerv[:, pl.ds(pl.multiple_of(h * HEAD, HEAD), HEAD)]
            for r in range(0, ROWS, BLK):
                acc = kw[REACH:REACH + 1, :] * dvx[h, pl.ds(HALF + r, BLK), :]
                for t in range(TAPS):
                    if t != REACH:
                        v = dvx[h, pl.ds(HALF + r - t + REACH, BLK), :]
                        acc = acc + (v * taps[TAPS - 1 - t, pl.ds(HALF + r, BLK), :]) * kw[t:t + 1, :]
                gfv[g, pl.ds(r, BLK), lanes] = acc.astype(BF16)
        return [local(dkv.at[g], o_gk.at[:, cols(g)]), local(gfv.at[g], o_gf.at[:, cols(g)])]

    order = [(0, 0), (1, 1), (2, 3), (3, 2)]
    groups = [(x + NX - k) % NX for _, k in order]
    outs = []
    stages = []

    w_forward(1)
    first, out = backward(0, groups[0])
    outs.append(out)
    stages.append(first)

    g_core.wait_recv()
    for i in range(NZ):
        part = gown[pl.ds(i * HEAD, HEAD), :] + gcore[pl.ds(i * HEAD, HEAD), :].astype(F32)
        gx[i] = part.astype(BF16).reshape(NX, 32, 512)
    g_x = [remote(gx.at[:, (x + k) % NX], gxr.at[k - 1], x_peer(k)) for k in (1, 3, 2)]

    w_forward(3)
    second, out = backward(1, groups[1])
    outs.append(out)
    stages.append(second)
    outs += finish(0, groups[0], stages[0])

    w_forward(2)
    third, out = backward(2, groups[2])
    outs.append(out)
    stages.append(third)
    outs += finish(1, groups[1], stages[1])

    for copy in g_x:
        copy.wait_recv()
    for i in range(NZ):
        part = gx[i, x].astype(F32)
        for k in range(NX - 1):
            part = part + gxr[k, i].astype(F32)
        gz[i] = part.astype(BF16)
    g_z = [remote(gz.at[(z + k) % NZ], gzr.at[k - 1], z_peer(k)) for k in range(1, NZ)]

    fourth, out = backward(3, groups[3])
    outs.append(out)
    stages.append(fourth)

    k_rs = [remote(kp.at[(e + k) % 8], kpr.at[k - 1], xc_peer(k)) for k in range(1, 8)]
    outs += finish(2, groups[2], stages[2])

    for copy in g_z:
        copy.wait_recv()
    part = gz[z].astype(F32)
    for k in range(NZ - 1):
        part = part + gzr[k].astype(F32)
    for s in range(nseq):
        for i in range(4):
            gs[s, pl.ds(2 * i, 2), :] = part[2 * s:2 * s + 2, i * HEAD:(i + 1) * HEAD]
    g_s = [remote(gs.at[(sq + k) % nseq], gsr.at[k - 1], seq_peer(k)) for k in range(1, nseq)]

    for copy in k_rs:
        copy.wait_recv()
    part = kp[e]
    for k in range(7):
        part = part + kpr[k]
    kz[...] = part
    k_z = [remote(kz, kzr.at[k - 1], z_peer(k)) for k in range(1, NZ)]

    outs += finish(3, groups[3], stages[3])

    for copy in k_z:
        copy.wait_recv()
    part = kz[...]
    for k in range(NZ - 1):
        part = part + kzr[k]
    ky[...] = part
    k_y = [remote(ky, kyr.at[k - 1], y_peer(k)) for k in range(1, NY)]

    lay[...] = dot(mixed[...], wfull[...], (1, 0)).astype(BF16)
    outs.append(local(lay, o_layer))

    for copy in k_y:
        copy.wait_recv()
    part = ky[...]
    for k in range(NY - 1):
        part = part + kyr[k]
    part = part * norm
    kall[e] = part
    kfin[...] = part
    k_ag = [remote(kfin, kall.at[e], xc_peer(k)) for k in range(1, 8)]

    for copy in g_s:
        copy.wait_recv()
    same = gs[sq]
    for k in range(2, nseq, 2):
        same = same + gsr[k - 1]
    cross = gsr[0]
    for k in range(3, nseq, 2):
        cross = cross + gsr[k - 1]
    low = jnp.where(c == 0, same, cross) * norm
    high = jnp.where(c == 0, cross, same) * norm
    for i in range(4):
        gwv[:, i * HEAD:(i + 1) * HEAD] = low[2 * i:2 * i + 2, :]
        gwv[:, 512 + i * HEAD:512 + (i + 1) * HEAD] = high[2 * i:2 * i + 2, :]
    outs.append(local(gwv, o_gw))

    for copy in k_ag:
        copy.wait_recv()
    for h in range(8):
        kout[:, h * HEAD:(h + 1) * HEAD] = kall[h, pl.ds(0, TAPS), :]
    outs.append(local(kout, o_gker))
    for copy in outs:
        copy.wait()
    for copy in sends:
        copy.wait_send()


def body(features, queries, key_rows, kernel_taps, out_weight, cotangent, lengths):
    norm = float(lax.axis_size("dp") * lax.axis_size("seq") * ROWS) ** -0.5
    any_spec = pl.BlockSpec(memory_space=pl.ANY)
    sheet = jax.ShapeDtypeStruct((ROWS, WIDTH), BF16)
    v = pltpu.VMEM
    scratch = [
        v((GROUPS, FEXT, PAIR), BF16),
        v((8, FEXT, HEAD), F32),
        v((GROUPS, EXT, PAIR), BF16),
        v((GROUPS, ROWS, PAIR), BF16),
        v((ROWS, WIDTH), BF16),
        v((TAPS, WIDTH), F32),
        v((FEXT, HEAD), jnp.int32),
        v((TAPS, EXT, HEAD), F32),
        v((2, BLK, SPAN), F32),
        v((GROUPS, EXT, PAIR), BF16),
        v((8, 2, BLK, SPAN), F32),
        v((ROWS, WIDTH), BF16),
        v((16, 64), BF16),
        v((16, 64), BF16),
        v((16, HEAD), BF16),
        v((16, WIDTH), BF16),
        v((WIDTH, WIDTH), BF16),
        v((WIDTH, 512), BF16),
        v((WIDTH, 512), F32),
        v((WIDTH, 512), BF16),
        v((NZ, NX, 32, 512), BF16),
        v((NX - 1, NZ, 32, 512), BF16),
        v((NZ, 32, 512), BF16),
        v((NZ - 1, 32, 512), BF16),
        v((16, 8, HEAD), F32),
        v((15, 8, HEAD), F32),
        v((2, WIDTH), F32),
        v((GROUPS, ROWS, PAIR), BF16),
        v((8, EXT, HEAD), F32),
        v((8, EXT, HEAD), F32),
        v((GROUPS, 2, HALF, PAIR), BF16),
        v((GROUPS, 2, FHALO, PAIR), BF16),
        v((GROUPS, 2, HALF, PAIR), BF16),
        v((GROUPS, 2, FHALO, PAIR), BF16),
        v((GROUPS, ROWS, PAIR), BF16),
        v((GROUPS, ROWS, PAIR), BF16),
        v((ROWS, WIDTH), BF16),
        v((8, 16, HEAD), F32),
        v((7, 16, HEAD), F32),
        v((16, HEAD), F32),
        v((NZ - 1, 16, HEAD), F32),
        v((16, HEAD), F32),
        v((NY - 1, 16, HEAD), F32),
        v((16, HEAD), F32),
        v((8, 16, HEAD), F32),
        v((TAPS, WIDTH), F32),
        pltpu.SemaphoreType.DMA((NSEM,)),
        pltpu.SemaphoreType.DMA((NSEM,)),
        pltpu.SemaphoreType.DMA((48,)),
    ]
    layer, grad_q, grad_k, grad_in, grad_kernel, grad_weight = pl.pallas_call(
        functools.partial(kernel, norm),
        out_shape=(
            sheet, sheet, sheet, sheet,
            jax.ShapeDtypeStruct((TAPS, WIDTH), F32),
            jax.ShapeDtypeStruct((2, WIDTH), F32),
        ),
        in_specs=[any_spec] * 6 + [pl.BlockSpec(memory_space=pltpu.SMEM)],
        out_specs=[any_spec] * 6,
        scratch_shapes=scratch,
        compiler_params=pltpu.CompilerParams(
            collective_id=0, has_side_effects=True, vmem_limit_bytes=56 * 1024 * 1024
        ),
        name="block",
    )(features[0], queries[0], key_rows[0], kernel_taps, out_weight, cotangent[0], lengths)
    return (layer[None], grad_q[None], grad_k[None], grad_in[None], grad_kernel, grad_weight)


def solution(mesh):
    sheet = P("dp", "seq", None)
    in_specs = (sheet, sheet, sheet, P(), P(None, "seq"), sheet, P("dp", None))
    out_specs = (sheet, sheet, sheet, sheet, P(), P(("dp", "seq"), None))
    return jax.shard_map(body, mesh=mesh, in_specs=in_specs, out_specs=out_specs, check_vma=False)
```

time: 503 us -> 94.8 us (0.19)
  waiting for transfers between devices: 301 us -> 0 us
  blocking collectives: 98.7 us -> 0 us
  Pallas kernels: 0 us -> 85.7 us
  starting transfers between devices: 24.8 us -> 0 us
  other arithmetic: 19.5 us -> 0 us
  matrix products: 19 us -> 0 us
  between operations: 16 us -> 0.66 us
  local copies, waits for them, and re-layouts: 23.2 us -> 8.14 us
    unnamed x3 -> x0, waiting for transfers between devices: 290 us -> none
    psum x1 -> x0, blocking collectives: 98.7 us -> none  [body(): grad_kernel = lax.psum(kernel_part, ('dp', 'seq')) * norm]
    pallas_call x0 -> x1, Pallas kernels: none -> 85.7 us  [body(): pl.pallas_call(functools.partial(kernel, norm), out_shape=(sheet, sheet,...]
    ppermute x8 -> x0, starting transfers between devices: 24.6 us -> none  [the longest x3 10.5 us: with_halo(): lax.ppermute(head, axis, [((i + 1) % count, i) for i in range(ends)])]
    dot_general x9 -> x0, matrix products: 19 us -> none  [the longest x1 5.08 us: backward_attention(): jnp.einsum('htu,thd->uhd', again_bf, back_h, preferred_element_type=jnp.f...]
    ppermute x8 -> x0, waiting for transfers between devices: 10.6 us -> none  [the longest x3 4.4 us: with_halo(): lax.ppermute(head, axis, [((i + 1) % count, i) for i in range(ends)])]
    another operation x5 -> x0, other arithmetic: 7.66 us -> none  [the longest x2 7.2 us: body(): paired = with_halo(jnp.stack([key_row, own_values]), (('seq', 1),), HALF)]
  transfers between devices with their start and end apart: 10 -> 0, of which waited for: 4 -> 0; matrix products, arithmetic and copies ran while one was open for 2% -> 0% of each run, Pallas kernels for 0% -> 0%
where the time goes in v1:
time: 94.8 us; the launch traced here: 94.5 us
  Pallas kernels  85.7 us (90%)
  local copies, waits for them, and re-layouts  8.14 us (9%)
    pallas_call x1, Pallas kernels, body(): pl.pallas_call(functools.partial(kernel, norm), out_shape=(sheet, sheet,...  85.7 us
    unnamed x17, local copies, waits for them, and re-layouts  8.14 us

profile of v1, /device:TPU:1, one launch (start us, length us, event | category | flops | bytes accessed | tf_op | source)
XLA Modules:
  0.0 94.5 jit_solution(6329166770574091645)
XLA Ops:
  0.6 1.7 %copy.13.wgt = bf16[1024,64]{1,0:T(8,128)(2,1)} copy(bf16[1024,64]{0,1:T(8,128)(2,1)} %param.11) | data formatting | bytes 262144 | tf_op args[4]
  2.4 85.7 %block.1 = (bf16[224,1024]{1,0:T(8,128)(2,1)}, bf16[224,1024]{1,0:T(8,128)(2,1)}, bf16[224,1024]{1,0:T(8,128)(2,1)}, bf16[224,1024]{1,0:T(8,128)(2,1)}, f32[9,1024]{1,0:T(8,128)}, /*index=5*/f32[2,1024]{1,0:T(2,128)}) custom-call(bf16[224,1024]{1,0:T(8,128)(2,1)} %bitcast.8, bf16[224,1024]{1,0:T(8,128)(2,1)} %bitcast.9, bf16[224,1024]{1,0:T(8,128)(2,1)} %bitcast.10, ...), custom_call_target="tpu_custom_call" | custom-call | tf_op jit(solution)/shard_map/block/pallas_call | solution.py:499
  88.1 0.0 copy-start.2
  88.1 1.9 %copy.20 = bf16[1,224,1024]{2,1,0:T(8,128)(2,1)} copy(bf16[1,224,1024]{2,1,0:T(8,128)(2,1)} %bitcast.15) | data formatting | bytes 917504
  89.9 0.0 copy-done.2
  89.9 0.0 copy-start.1
  89.9 0.8 copy.21
  90.7 0.4 copy-done.1
  91.1 0.0 copy-start
  91.1 0.8 copy.22
  91.9 0.4 copy-done
  92.3 0.0 copy-start.3
  92.3 0.8 copy.23
  93.1 0.1 copy-done.3
  93.2 0.0 copy-start.4
  93.2 0.6 copy.24
  93.8 0.1 copy-done.4
  93.9 0.6 copy.25
Async XLA Ops:
  88.1 1.9 %copy-start.2 = (bf16[224,1024]{1,0:T(8,128)(2,1)S(1)}, bf16[224,1024]{1,0:T(8,128)(2,1)}, u32[]{:S(2)}) copy-start(bf16[224,1024]{1,0:T(8,128)(2,1)} %get-tuple-element.13) | copy-start | bytes 1376260
  89.9 1.2 %copy-start.1 = (bf16[224,1024]{1,0:T(8,128)(2,1)S(1)}, bf16[224,1024]{1,0:T(8,128)(2,1)}, u32[]{:S(2)}) copy-start(bf16[224,1024]{1,0:T(8,128)(2,1)} %get-tuple-element.14) | copy-start | bytes 1376260
  91.1 1.2 %copy-start = (bf16[224,1024]{1,0:T(8,128)(2,1)S(1)}, bf16[224,1024]{1,0:T(8,128)(2,1)}, u32[]{:S(2)}) copy-start(bf16[224,1024]{1,0:T(8,128)(2,1)} %get-tuple-element.15) | copy-start | bytes 1376260
  92.3 0.9 copy-start.3
  93.2 0.7 copy-start.4

commit v2 on v1

v2 whole, which is shorter than its diff:
```python
import functools
import math

import jax
import jax.numpy as jnp
from jax import lax
from jax.experimental import pallas as pl
from jax.experimental.pallas import tpu as pltpu
from jax.sharding import PartitionSpec as P

MESH = pl.DeviceIdType.MESH
F32 = jnp.float32
BF16 = jnp.bfloat16

HALF = 128
TAPS = 9
REACH = 4
RIM = 16
UTT = 16
ROWS = 224
WIDTH = 1024
HEAD = 128
PAIR = 256
GROUPS = 4
NX = 4
NZ = 8
NY = 8
EXT = ROWS + 2 * HALF
FEXT = EXT + 2 * RIM
FHALO = HALF + RIM
BLK = 112
SPAN = 384
BLKOFF = 96
NSEM = 160
KROWS = 48


def dot(a, b, contract):
    return lax.dot_general(a, b, ((contract[:1], contract[1:]), ((), ())), preferred_element_type=F32)


def kernel(
    norm,
    feat, qry, key, ker, wgt, cot, lens,
    o_layer, o_gq, o_gk, o_gf, o_gker, o_gw,
    fext, fs, kext, qv, cotv, kerv, segs, taps, bias, vext, probs, mixed, backv,
    w1, wt,
    gsend, gown, gcore, ga, gar, gb, gbr, gza, gzar, gxb, gxbr, gs, gsr, gfin, gsib, gwv,
    dqv, dkx, dvx, dks, dvs, dkr, dvr, dkv, gfv, lay,
    kp, kpr, kx, kz, ky, kfin, kout,
    ss, rs, ls,
):
    dp = lax.axis_index("dp")
    sq = lax.axis_index("seq")
    z, x = dp // NX, dp % NX
    y, c = sq // 2, sq % 2
    nseq = 2 * NY
    seqlen = nseq * ROWS
    offset = sq * ROWS

    def dev(d, s):
        return {"dp": d, "seq": s}

    sib = dev(dp, sq + 1 - 2 * c)
    right = dev(dp, (sq + 1) % nseq)
    left = dev(dp, (sq + nseq - 1) % nseq)

    def y_peer(k):
        return dev(dp, ((y + k) % NY) * 2 + c)

    def z_peer(k):
        return dev(((z + k) % NZ) * NX + x, sq)

    def x_peer(k):
        return dev(z * NX + (x + k) % NX, sq)

    x_order = (1, 3, 2)
    ring_order = (4, 3, 5, 2, 6, 1, 7)

    barrier = pltpu.get_barrier_semaphore()
    friends = [left, right]
    friends += [y_peer(k) for k in range(1, NY)]
    friends += [z_peer(k) for k in range(1, NZ)]
    friends += [x_peer(k) for k in range(1, NX)]
    for friend in friends:
        pl.semaphore_signal(barrier, inc=1, device_id=friend, device_id_type=MESH)

    used = [0, 0]
    sends = []

    def remote(src, dst, device):
        index = used[0]
        used[0] += 1
        copy = pltpu.make_async_remote_copy(
            src_ref=src, dst_ref=dst, send_sem=ss.at[index], recv_sem=rs.at[index],
            device_id=device, device_id_type=MESH,
        )
        copy.start()
        sends.append(copy)
        return copy

    def local(src, dst):
        index = used[1]
        used[1] += 1
        copy = pltpu.make_async_copy(src, dst, ls.at[index])
        copy.start()
        return copy

    def received(copies):
        for copy in copies:
            copy.wait_recv()

    def cols(g):
        return pl.ds(g * PAIR, PAIR)

    zcol = pl.ds(pl.multiple_of(z * HEAD, HEAD), HEAD)
    w_src = wgt.at[pl.ds(pl.multiple_of(x * 16, 16), 16), zcol]
    w_own = local(w_src, w1.at[y])
    loads = []
    for g in range(GROUPS):
        loads.append([
            local(feat.at[:, cols(g)], fext.at[g, pl.ds(FHALO, ROWS)]),
            local(key.at[:, cols(g)], kext.at[g, pl.ds(HALF, ROWS)]),
            local(qry.at[:, cols(g)], qv.at[g]),
        ])
    ker_in = local(ker, kerv)
    cot_in = local(cot, cotv)

    pl.semaphore_wait(barrier, len(friends))

    w_y = [remote(w_src, w1.at[y], y_peer(k)) for k in ring_order]
    halos = []
    for g in range(GROUPS):
        halos.append([
            remote(feat.at[pl.ds(ROWS - FHALO, FHALO), cols(g)], fext.at[g, pl.ds(0, FHALO)], right),
            remote(feat.at[pl.ds(0, FHALO), cols(g)], fext.at[g, pl.ds(FHALO + ROWS, FHALO)], left),
            remote(key.at[pl.ds(ROWS - HALF, HALF), cols(g)], kext.at[g, pl.ds(0, HALF)], right),
            remote(key.at[pl.ds(0, HALF), cols(g)], kext.at[g, pl.ds(HALF + ROWS, HALF)], left),
        ])

    bounds = []
    total = lens[0, 0]
    bounds.append(total)
    for k in range(1, UTT):
        total = total + lens[0, k]
        bounds.append(total)

    def segment(pos):
        seg = jnp.where(pos < 0, -1, 0)
        for bound in bounds:
            seg = seg + jnp.where(pos >= bound, 1, 0)
        return seg

    for r in range(0, FEXT, 64):
        pos = offset - FHALO + r + lax.broadcasted_iota(jnp.int32, (64, HEAD), 0)
        segs[pl.ds(r, 64), :] = segment(pos)
    for r in range(0, EXT, 96):
        center = segs[pl.ds(RIM + r, 96), :]
        for j in range(TAPS):
            near = segs[pl.ds(RIM - REACH + j + r, 96), :]
            taps[j, pl.ds(r, 96), :] = jnp.where(center == near, 1.0, 0.0).astype(F32)
    for b in range(2):
        colpos = offset - HALF + BLKOFF * b + lax.broadcasted_iota(jnp.int32, (8, SPAN), 1)
        seg_col = segment(colpos)[0:1, :]
        seg_row = segs[pl.ds(FHALO + BLK * b, BLK), :]
        seg_row = jnp.concatenate([seg_row] * (SPAN // HEAD), axis=1)
        gap = (
            lax.broadcasted_iota(jnp.int32, (BLK, SPAN), 0) + (BLK * b + HALF - BLKOFF * b)
            - lax.broadcasted_iota(jnp.int32, (BLK, SPAN), 1)
        )
        ok = (seg_row == seg_col) & (gap <= HALF) & (gap >= -HALF)
        bias[b] = jnp.where(ok, 0.0, -jnp.inf).astype(F32)

    w_own.wait()
    received(w_y)
    near_y, far_y = pl.ds(0, 6), pl.ds(6, 2)
    wt[near_y, c, x, :, zcol] = w1[near_y]
    wt[far_y, c, x, :, zcol] = w1[far_y]
    w_za = [remote(w1.at[near_y], wt.at[near_y, c, x, :, zcol], z_peer(k)) for k in ring_order]
    w_xb = [remote(w1.at[far_y], wt.at[far_y, c, x, :, zcol], x_peer(k)) for k in x_order]

    scale = HEAD ** -0.5
    scale2 = scale * math.log2(math.e)
    sib_cols = pl.ds(pl.multiple_of((1 - c) * 512, 512), 512)
    own_cols = pl.ds(pl.multiple_of(c * 512, 512), 512)

    def forward(g):
        for copy in loads[g]:
            copy.wait()
        received(halos[g])
        for j in range(2):
            lanes = pl.ds(j * HEAD, HEAD)
            h = 2 * g + j
            fs[h] = fext[g, :, lanes].astype(F32)
            kw = kerv[:, pl.ds(h * HEAD, HEAD)]
            for r in range(0, EXT, 96):
                acc = kw[REACH:REACH + 1, :] * fs[h, pl.ds(r + RIM, 96), :]
                for t in range(TAPS):
                    if t != REACH:
                        f = fs[h, pl.ds(r + RIM - REACH + t, 96), :]
                        acc = acc + (f * taps[t, pl.ds(r, 96), :]) * kw[t:t + 1, :]
                vext[g, pl.ds(r, 96), lanes] = acc.astype(BF16)
        for j in range(2):
            lanes = pl.ds(j * HEAD, HEAD)
            h = 2 * g + j
            for b in range(2):
                qb = qv[g, pl.ds(BLK * b, BLK), lanes]
                kb = kext[g, pl.ds(BLKOFF * b, SPAN), lanes]
                s = dot(qb, kb, (1, 1)) * scale2 + bias[b]
                top = jnp.max(s, axis=1, keepdims=True)
                ex = jnp.exp2(s - top)
                p = ex * (1.0 / jnp.sum(ex, axis=1, keepdims=True))
                probs[h, b] = p
                vb = vext[g, pl.ds(BLKOFF * b, SPAN), lanes]
                mixed[pl.ds(BLK * b, BLK), pl.ds(h * HEAD, HEAD)] = dot(p.astype(BF16), vb, (1, 0)).astype(BF16)

    g_core = [None] * GROUPS
    g_xa = []

    def weight_term(g):
        mb = mixed[:, cols(g)]
        gsend[g] = dot(mb, cotv[:, sib_cols], (0, 0)).astype(BF16)
        g_core[g] = remote(gsend.at[g], gcore.at[g], sib)
        gown[g] = dot(mb, cotv[:, own_cols], (0, 0))

    def weight_along_x(g):
        g_core[g].wait_recv()
        for i in range(2):
            half = pl.ds(i * HEAD, HEAD)
            part = (gown[g, half, :] + gcore[g, half, :].astype(F32)).astype(BF16).reshape(NX, 32, 512)
            ga[2 * g + i] = part[:, :, :384]
            gb[2 * g + i] = part[:, :, 384:]
        two = pl.ds(2 * g, 2)
        for k in x_order:
            g_xa.append(remote(ga.at[two, (x + k) % NX], gar.at[k - 1, two], x_peer(k)))

    ker_in.wait()
    forward(0)
    cot_in.wait()
    weight_term(0)

    received(w_za)
    w_s = [remote(wt.at[near_y, c, x], wt.at[near_y, c, x], sib)]
    w_xa = {k: remote(wt.at[near_y, c, x], wt.at[near_y, c, x], x_peer(k)) for k in x_order}
    received(w_xb)
    w_zb = [remote(wt.at[far_y, c, :, :, zcol], wt.at[far_y, c, :, :, zcol], z_peer(k)) for k in ring_order]

    forward(1)
    weight_term(1)
    weight_along_x(0)
    forward(2)
    weight_term(2)
    weight_along_x(1)
    forward(3)
    weight_term(3)
    weight_along_x(2)

    received(w_zb)
    w_s.append(remote(wt.at[far_y, c], wt.at[far_y, c], sib))
    for k in x_order:
        w_xa[k].wait_recv()
        there = (x + NX - k) % NX
        w_s.append(remote(wt.at[near_y, c, there], wt.at[near_y, c, there], sib))

    weight_along_x(3)
    g_zb = [remote(gb.at[(z + k) % NZ], gbr.at[k - 1], z_peer(k)) for k in ring_order]

    received(w_s)
    wide = wt[...].reshape(WIDTH, WIDTH)
    backv[...] = dot(cotv[...], wide, (1, 0)).astype(BF16)

    dv_halos = []
    for g in range(GROUPS):
        for j in range(2):
            lanes = pl.ds(j * HEAD, HEAD)
            h = 2 * g + j
            first, second = [
                dot(probs[h, b].astype(BF16), backv[pl.ds(BLK * b, BLK), pl.ds(h * HEAD, HEAD)], (0, 0)) for b in range(2)
            ]
            dvx[h, pl.ds(0, BLKOFF), :] = first[:BLKOFF]
            dvx[h, pl.ds(BLKOFF, SPAN - BLKOFF), :] = first[BLKOFF:] + second[:SPAN - BLKOFF]
            dvx[h, pl.ds(SPAN, EXT - SPAN), :] = second[SPAN - BLKOFF:]
            sums = [jnp.zeros((8, HEAD), F32) for _ in range(TAPS)]
            for r in range(0, EXT, 96):
                gv = dvx[h, pl.ds(r, 96), :]
                for t in range(TAPS):
                    term = gv * fs[h, pl.ds(r + RIM - REACH + t, 96), :]
                    if t != REACH:
                        term = term * taps[t, pl.ds(r, 96), :]
                    sums[t] = sums[t] + jnp.sum(term.reshape(12, 8, HEAD), axis=0)
            rows = jnp.concatenate([jnp.sum(v, axis=0, keepdims=True) for v in sums], axis=0)
            kp[h // 4, pl.ds((h % 4) * TAPS, TAPS), :] = rows
            dvs[g, 0, :, lanes] = dvx[h, pl.ds(0, FHALO), :].astype(BF16)
            dvs[g, 1, :, lanes] = dvx[h, pl.ds(EXT - FHALO, FHALO), :].astype(BF16)
    k_sib = remote(kp.at[1 - c], kpr, sib)
    for g in range(GROUPS):
        dv_halos.append([
            remote(dvs.at[g, 0], dvr.at[g, 0], left),
            remote(dvs.at[g, 1], dvr.at[g, 1], right),
        ])

    outs = []
    dk_halos = []

    def backward(g):
        for j in range(2):
            lanes = pl.ds(j * HEAD, HEAD)
            h = 2 * g + j
            bh = backv[:, pl.ds(h * HEAD, HEAD)]
            mh = mixed[:, pl.ds(h * HEAD, HEAD)]
            inner = jnp.sum(bh.astype(F32) * mh.astype(F32), axis=1, keepdims=True)
            parts = []
            for b in range(2):
                rows = slice(BLK * b, BLK * b + BLK)
                kb = kext[g, pl.ds(BLKOFF * b, SPAN), lanes]
                vb = vext[g, pl.ds(BLKOFF * b, SPAN), lanes]
                qb = qv[g, pl.ds(BLK * b, BLK), lanes]
                ds = (probs[h, b] * (dot(bh[rows], vb, (1, 1)) - inner[rows])).astype(BF16)
                dqv[g, pl.ds(BLK * b, BLK), lanes] = (dot(ds, kb, (1, 0)) * scale).astype(BF16)
                parts.append(dot(ds, qb, (0, 0)) * scale)
            first, second = parts
            dkx[h, pl.ds(0, BLKOFF), :] = first[:BLKOFF]
            dkx[h, pl.ds(BLKOFF, SPAN - BLKOFF), :] = first[BLKOFF:] + second[:SPAN - BLKOFF]
            dkx[h, pl.ds(SPAN, EXT - SPAN), :] = second[SPAN - BLKOFF:]
            dks[g, 0, :, lanes] = dkx[h, pl.ds(0, HALF), :].astype(BF16)
            dks[g, 1, :, lanes] = dkx[h, pl.ds(EXT - HALF, HALF), :].astype(BF16)
        dk_halos.append([
            remote(dks.at[g, 0], dkr.at[g, 0], left),
            remote(dks.at[g, 1], dkr.at[g, 1], right),
        ])
        outs.append(local(dqv.at[g], o_gq.at[:, cols(g)]))

    def finish(g):
        received(dv_halos[g])
        for j in range(2):
            lanes = pl.ds(j * HEAD, HEAD)
            h = 2 * g + j
            dvx[h, pl.ds(HALF - RIM, FHALO), :] += dvr[g, 1, :, lanes].astype(F32)
            dvx[h, pl.ds(ROWS, FHALO), :] += dvr[g, 0, :, lanes].astype(F32)
            kw = kerv[:, pl.ds(h * HEAD, HEAD)]
            for r in range(0, ROWS, BLK):
                acc = kw[REACH:REACH + 1, :] * dvx[h, pl.ds(HALF + r, BLK), :]
                for t in range(TAPS):
                    if t != REACH:
                        v = dvx[h, pl.ds(HALF + r - t + REACH, BLK), :]
                        acc = acc + (v * taps[TAPS - 1 - t, pl.ds(HALF + r, BLK), :]) * kw[t:t + 1, :]
                gfv[g, pl.ds(r, BLK), lanes] = acc.astype(BF16)
        outs.append(local(gfv.at[g], o_gf.at[:, cols(g)]))
        received(dk_halos[g])
        for j in range(2):
            lanes = pl.ds(j * HEAD, HEAD)
            h = 2 * g + j
            dkx[h, pl.ds(HALF, HALF), :] += dkr[g, 1, :, lanes].astype(F32)
            dkx[h, pl.ds(ROWS, HALF), :] += dkr[g, 0, :, lanes].astype(F32)
            dkv[g, :, lanes] = dkx[h, pl.ds(HALF, ROWS), :].astype(BF16)
        outs.append(local(dkv.at[g], o_gk.at[:, cols(g)]))

    backward(0)
    k_sib.wait_recv()
    kx[x] = kp[c] + kpr[...]
    k_x = [remote(kx.at[x], kx.at[x], x_peer(k)) for k in x_order]

    received(g_xa)
    for i in range(NZ):
        part = ga[i, x].astype(F32)
        for k in range(NX - 1):
            part = part + gar[k, i].astype(F32)
        gza[i] = part.astype(BF16)
    g_za = [remote(gza.at[(z + k) % NZ], gzar.at[k - 1], z_peer(k)) for k in ring_order]
    received(g_zb)
    for i in range(NX):
        part = gb[z, i].astype(F32)
        for k in range(NZ - 1):
            part = part + gbr[k, i].astype(F32)
        gxb[i] = part.astype(BF16)
    g_xb = [remote(gxb.at[(x + k) % NX], gxbr.at[k - 1], x_peer(k)) for k in x_order]

    backward(1)
    received(k_x)
    kz[z] = (kx[0] + kx[1] + kx[2] + kx[3]).astype(BF16)
    k_z = [remote(kz.at[z], kz.at[z], z_peer(k)) for k in ring_order]

    backward(2)
    backward(3)
    finish(0)

    received(k_z)
    part = kz[0].astype(F32)
    for k in range(1, NZ):
        part = part + kz[k].astype(F32)
    ky[y] = part.astype(BF16)
    k_y = [remote(ky.at[y], ky.at[y], y_peer(k)) for k in ring_order]

    finish(1)

    received(g_za)
    received(g_xb)
    part = gza[z].astype(F32)
    for k in range(NZ - 1):
        part = part + gzar[k].astype(F32)
    last = gxb[x].astype(F32)
    for k in range(NX - 1):
        last = last + gxbr[k].astype(F32)
    part = jnp.concatenate([part, last], axis=1)
    for s in range(NY):
        for i in range(4):
            gs[s, pl.ds(4 * i, 4), :] = part[4 * s:4 * s + 4, i * HEAD:(i + 1) * HEAD]
    g_y = [remote(gs.at[(y + k) % NY], gsr.at[k - 1], y_peer(k)) for k in ring_order]

    finish(2)
    finish(3)
    lay[...] = dot(mixed[...], wt[...].reshape(WIDTH, WIDTH), (1, 1)).astype(BF16)
    outs.append(local(lay, o_layer))

    received(k_y)
    part = ky[0].astype(F32)
    for k in range(1, NY):
        part = part + ky[k].astype(F32)
    kfin[c] = part * norm
    k_last = remote(kfin.at[c], kfin.at[c], sib)

    received(g_y)
    part = gs[y]
    for k in range(NY - 1):
        part = part + gsr[k]
    gfin[...] = part * norm
    g_last = remote(gfin, gsib, sib)

    k_last.wait_recv()
    for h in range(8):
        kout[:, h * HEAD:(h + 1) * HEAD] = kfin[h // 4, pl.ds((h % 4) * TAPS, TAPS), :]
    outs.append(local(kout, o_gker))

    g_last.wait_recv()
    mine, theirs = gfin[...], gsib[...]
    low = jnp.where(c == 0, mine, theirs)
    high = jnp.where(c == 0, theirs, mine)
    for n, half in enumerate((low, high)):
        for i in range(4):
            rows = jnp.where(c == 0, half[4 * i:4 * i + 2, :], half[4 * i + 2:4 * i + 4, :])
            gwv[:, n * 512 + i * HEAD:n * 512 + (i + 1) * HEAD] = rows
    outs.append(local(gwv, o_gw))

    for copy in outs:
        copy.wait()
    for copy in sends:
        copy.wait_send()


def hand_over(*refs):
    given, out, held, sem = refs[:6], refs[6:12], refs[12:18], refs[18]
    loads = [pltpu.make_async_copy(given[i], held[i], sem.at[i]) for i in range(6)]
    stores = [pltpu.make_async_copy(held[i], out[i], sem.at[6 + i]) for i in range(6)]
    for copy in loads:
        copy.start()
    for load, store in zip(loads, stores):
        load.wait()
        store.start()
    for copy in stores:
        copy.wait()


def body(features, queries, key_rows, kernel_taps, out_weight, cotangent, lengths):
    norm = float(lax.axis_size("dp") * lax.axis_size("seq") * ROWS) ** -0.5
    any_spec = pl.BlockSpec(memory_space=pl.ANY)
    sheet = jax.ShapeDtypeStruct((ROWS, WIDTH), BF16)
    v = pltpu.VMEM
    scratch = [
        v((GROUPS, FEXT, PAIR), BF16),
        v((8, FEXT, HEAD), F32),
        v((GROUPS, EXT, PAIR), BF16),
        v((GROUPS, ROWS, PAIR), BF16),
        v((ROWS, WIDTH), BF16),
        v((TAPS, WIDTH), F32),
        v((FEXT, HEAD), jnp.int32),
        v((TAPS, EXT, HEAD), F32),
        v((2, BLK, SPAN), F32),
        v((GROUPS, EXT, PAIR), BF16),
        v((8, 2, BLK, SPAN), F32),
        v((ROWS, WIDTH), BF16),
        v((ROWS, WIDTH), BF16),
        v((NY, 16, HEAD), BF16),
        v((NY, 2, NX, 16, WIDTH), BF16),
        v((GROUPS, PAIR, 512), BF16),
        v((GROUPS, PAIR, 512), F32),
        v((GROUPS, PAIR, 512), BF16),
        v((NZ, NX, 32, 384), BF16),
        v((NX - 1, NZ, 32, 384), BF16),
        v((NZ, NX, 32, 128), BF16),
        v((NZ - 1, NX, 32, 128), BF16),
        v((NZ, 32, 384), BF16),
        v((NZ - 1, 32, 384), BF16),
        v((NX, 32, 128), BF16),
        v((NX - 1, 32, 128), BF16),
        v((NY, 16, HEAD), F32),
        v((NY - 1, 16, HEAD), F32),
        v((16, HEAD), F32),
        v((16, HEAD), F32),
        v((2, WIDTH), F32),
        v((GROUPS, ROWS, PAIR), BF16),
        v((8, EXT, HEAD), F32),
        v((8, EXT, HEAD), F32),
        v((GROUPS, 2, HALF, PAIR), BF16),
        v((GROUPS, 2, FHALO, PAIR), BF16),
        v((GROUPS, 2, HALF, PAIR), BF16),
        v((GROUPS, 2, FHALO, PAIR), BF16),
        v((GROUPS, ROWS, PAIR), BF16),
        v((GROUPS, ROWS, PAIR), BF16),
        v((ROWS, WIDTH), BF16),
        v((2, KROWS, HEAD), F32),
        v((KROWS, HEAD), F32),
        v((NX, KROWS, HEAD), F32),
        v((NZ, KROWS, HEAD), BF16),
        v((NY, KROWS, HEAD), BF16),
        v((2, KROWS, HEAD), F32),
        v((TAPS, WIDTH), F32),
        pltpu.SemaphoreType.DMA((NSEM,)),
        pltpu.SemaphoreType.DMA((NSEM,)),
        pltpu.SemaphoreType.DMA((48,)),
    ]
    shapes = (
        sheet, sheet, sheet, sheet,
        jax.ShapeDtypeStruct((TAPS, WIDTH), F32),
        jax.ShapeDtypeStruct((2, WIDTH), F32),
    )
    results = pl.pallas_call(
        functools.partial(kernel, norm),
        out_shape=shapes,
        in_specs=[any_spec] * 6 + [pl.BlockSpec(memory_space=pltpu.SMEM)],
        out_specs=[any_spec] * 6,
        scratch_shapes=scratch,
        compiler_params=pltpu.CompilerParams(
            collective_id=0, has_side_effects=True, vmem_limit_bytes=56 * 1024 * 1024
        ),
        name="block",
    )(features[0], queries[0], key_rows[0], kernel_taps, out_weight.T, cotangent[0], lengths)
    layer, grad_q, grad_k, grad_in, grad_kernel, grad_weight = pl.pallas_call(
        hand_over,
        out_shape=shapes,
        in_specs=[any_spec] * 6,
        out_specs=[any_spec] * 6,
        scratch_shapes=[v(shape.shape, shape.dtype) for shape in shapes] + [pltpu.SemaphoreType.DMA((12,))],
        name="hand_over",
    )(*results)
    return (layer[None], grad_q[None], grad_k[None], grad_in[None], grad_kernel, grad_weight)


def solution(mesh):
    sheet = P("dp", "seq", None)
    in_specs = (sheet, sheet, sheet, P(), P(None, "seq"), sheet, P("dp", None))
    out_specs = (sheet, sheet, sheet, sheet, P(), P(("dp", "seq"), None))
    return jax.shard_map(body, mesh=mesh, in_specs=in_specs, out_specs=out_specs, check_vma=False)
```

time: 94.8 us -> 67.4 us (0.71)
  Pallas kernels: 85.7 us -> 66.4 us
  local copies, waits for them, and re-layouts: 8.14 us -> 0 us
    pallas_call x1 -> x2, Pallas kernels: 85.7 us -> 66.4 us  [the longest x1 64.1 us: body(): pl.pallas_call(functools.partial(kernel, norm), out_shape=shapes, in_spec...]
    unnamed x17 -> x0, local copies, waits for them, and re-layouts: 8.14 us -> none
where the time goes in v2:
time: 67.4 us; the launch traced here: 67.2 us
  Pallas kernels  66.4 us (99%)
  between operations  0.8 us (1%)
    pallas_call x1, Pallas kernels, body(): pl.pallas_call(functools.partial(kernel, norm), out_shape=shapes, in_spec...  64.1 us
    pallas_call x1, Pallas kernels, body(): pl.pallas_call(hand_over, out_shape=shapes, in_specs=[any_spec] * 6, out_...  2.36 us

profile of v2, /device:TPU:1, one launch (start us, length us, event | category | flops | bytes accessed | tf_op | source)
XLA Modules:
  0.0 67.2 jit_solution(17422777613179786144)
XLA Ops:
  0.6 64.1 %block.1 = (bf16[224,1024]{1,0:T(8,128)(2,1)}, bf16[224,1024]{1,0:T(8,128)(2,1)}, bf16[224,1024]{1,0:T(8,128)(2,1)}, bf16[224,1024]{1,0:T(8,128)(2,1)}, f32[9,1024]{1,0:T(8,128)}, /*index=5*/f32[2,1024]{1,0:T(2,128)}) custom-call(bf16[224,1024]{1,0:T(8,128)(2,1)} %bitcast.9, bf16[224,1024]{1,0:T(8,128)(2,1)} %bitcast.10, bf16[224,1024]{1,0:T(8,128)(2,1)} %bitcast.11, ...), custom_call_target="tpu_custom_call" | custom-call | tf_op jit(solution)/shard_map/block/pallas_call | solution.py:526
  64.7 2.4 %hand_over.1 = (bf16[224,1024]{1,0:T(8,128)(2,1)}, bf16[224,1024]{1,0:T(8,128)(2,1)}, bf16[224,1024]{1,0:T(8,128)(2,1)}, bf16[224,1024]{1,0:T(8,128)(2,1)}, f32[9,1024]{1,0:T(8,128)}, /*index=5*/f32[2,1024]{1,0:T(2,128)}) custom-call(bf16[224,1024]{1,0:T(8,128)(2,1)} %get-tuple-element.18.refs_0_, bf16[224,1024]{1,0:T(8,128)(2,1)} %get-tuple-element.19.refs_1_, ...), custom_call_target="tpu_custom_call" | custom-call | tf_op jit(solution)/shard_map/hand_over/pallas_call | solution.py:537

commit v3 on v2

--- a/solution.py
+++ b/solution.py
@@ -116,6 +116,9 @@
     zcol = pl.ds(pl.multiple_of(z * HEAD, HEAD), HEAD)
     w_src = wgt.at[pl.ds(pl.multiple_of(x * 16, 16), 16), zcol]
     w_own = local(w_src, w1.at[y])
+    far = (x + 2) % NX
+    far_src = wgt.at[pl.ds(pl.multiple_of(far * 16, 16), 16), :]
+    far_own = local(far_src, wt.at[y, c, far])
     loads = []
     for g in range(GROUPS):
         loads.append([
@@ -137,6 +140,8 @@
             remote(key.at[pl.ds(ROWS - HALF, HALF), cols(g)], kext.at[g, pl.ds(0, HALF)], right),
             remote(key.at[pl.ds(0, HALF), cols(g)], kext.at[g, pl.ds(HALF + ROWS, HALF)], left),
         ])
+
+    w_far = [remote(far_src, wt.at[y, c, far], y_peer(k)) for k in ring_order]
 
     bounds = []
     total = lens[0, 0]
@@ -173,11 +178,8 @@
 
     w_own.wait()
     received(w_y)
-    near_y, far_y = pl.ds(0, 6), pl.ds(6, 2)
-    wt[near_y, c, x, :, zcol] = w1[near_y]
-    wt[far_y, c, x, :, zcol] = w1[far_y]
-    w_za = [remote(w1.at[near_y], wt.at[near_y, c, x, :, zcol], z_peer(k)) for k in ring_order]
-    w_xb = [remote(w1.at[far_y], wt.at[far_y, c, x, :, zcol], x_peer(k)) for k in x_order]
+    wt[:, c, x, :, zcol] = w1[...]
+    w_z = [remote(w1, wt.at[:, c, x, :, zcol], z_peer(k)) for k in ring_order]
 
     scale = HEAD ** -0.5
     scale2 = scale * math.log2(math.e)
@@ -239,11 +241,14 @@
     cot_in.wait()
     weight_term(0)
 
-    received(w_za)
-    w_s = [remote(wt.at[near_y, c, x], wt.at[near_y, c, x], sib)]
-    w_xa = {k: remote(wt.at[near_y, c, x], wt.at[near_y, c, x], x_peer(k)) for k in x_order}
-    received(w_xb)
-    w_zb = [remote(wt.at[far_y, c, :, :, zcol], wt.at[far_y, c, :, :, zcol], z_peer(k)) for k in ring_order]
+    w_s = []
+
+    def to_sibling(there):
+        w_s.append(remote(wt.at[:, c, there], wt.at[:, c, there], sib))
+
+    received(w_z)
+    w_x = {k: remote(wt.at[:, c, x], wt.at[:, c, x], x_peer(k)) for k in (1, 3)}
+    to_sibling(x)
 
     forward(1)
     weight_term(1)
@@ -255,15 +260,15 @@
     weight_term(3)
     weight_along_x(2)
 
-    received(w_zb)
-    w_s.append(remote(wt.at[far_y, c], wt.at[far_y, c], sib))
-    for k in x_order:
-        w_xa[k].wait_recv()
-        there = (x + NX - k) % NX
-        w_s.append(remote(wt.at[near_y, c, there], wt.at[near_y, c, there], sib))
-
     weight_along_x(3)
     g_zb = [remote(gb.at[(z + k) % NZ], gbr.at[k - 1], z_peer(k)) for k in ring_order]
+
+    far_own.wait()
+    received(w_far)
+    to_sibling(far)
+    for k in (1, 3):
+        w_x[k].wait_recv()
+        to_sibling((x + NX - k) % NX)
 
     received(w_s)
     wide = wt[...].reshape(WIDTH, WIDTH)

time: 67.4 us -> 65.1 us (0.966)
  Pallas kernels: 66.4 us -> 64.1 us
    pallas_call x1, Pallas kernels: 64.1 us -> 61.7 us  [body(): pl.pallas_call(functools.partial(kernel, norm), out_shape=shapes, in_spec...]
where the time goes in v3:
time: 65.1 us; the launch traced here: 64.9 us
  Pallas kernels  64.1 us (98%)
  between operations  0.8 us (1%)
    pallas_call x1, Pallas kernels, body(): pl.pallas_call(functools.partial(kernel, norm), out_shape=shapes, in_spec...  61.7 us
    pallas_call x1, Pallas kernels, body(): pl.pallas_call(hand_over, out_shape=shapes, in_specs=[any_spec] * 6, out_...  2.36 us

profile of v3, /device:TPU:1, one launch (start us, length us, event | category | flops | bytes accessed | tf_op | source)
XLA Modules:
  0.0 64.9 jit_solution(993723344535116451)
XLA Ops:
  0.6 61.7 %block.1 = (bf16[224,1024]{1,0:T(8,128)(2,1)}, bf16[224,1024]{1,0:T(8,128)(2,1)}, bf16[224,1024]{1,0:T(8,128)(2,1)}, bf16[224,1024]{1,0:T(8,128)(2,1)}, f32[9,1024]{1,0:T(8,128)}, /*index=5*/f32[2,1024]{1,0:T(2,128)}) custom-call(bf16[224,1024]{1,0:T(8,128)(2,1)} %bitcast.9, bf16[224,1024]{1,0:T(8,128)(2,1)} %bitcast.10, bf16[224,1024]{1,0:T(8,128)(2,1)} %bitcast.11, ...), custom_call_target="tpu_custom_call" | custom-call | tf_op jit(solution)/shard_map/block/pallas_call | solution.py:531
  62.4 2.4 %hand_over.1 = (bf16[224,1024]{1,0:T(8,128)(2,1)}, bf16[224,1024]{1,0:T(8,128)(2,1)}, bf16[224,1024]{1,0:T(8,128)(2,1)}, bf16[224,1024]{1,0:T(8,128)(2,1)}, f32[9,1024]{1,0:T(8,128)}, /*index=5*/f32[2,1024]{1,0:T(2,128)}) custom-call(bf16[224,1024]{1,0:T(8,128)(2,1)} %get-tuple-element.18.refs_0_, bf16[224,1024]{1,0:T(8,128)(2,1)} %get-tuple-element.19.refs_1_, ...), custom_call_target="tpu_custom_call" | custom-call | tf_op jit(solution)/shard_map/hand_over/pallas_call | solution.py:542

commit v4 on v3

--- a/solution.py
+++ b/solution.py
@@ -241,6 +241,10 @@
     cot_in.wait()
     weight_term(0)
 
+    forward(1)
+    weight_term(1)
+    weight_along_x(0)
+
     w_s = []
 
     def to_sibling(there):
@@ -250,9 +254,6 @@
     w_x = {k: remote(wt.at[:, c, x], wt.at[:, c, x], x_peer(k)) for k in (1, 3)}
     to_sibling(x)
 
-    forward(1)
-    weight_term(1)
-    weight_along_x(0)
     forward(2)
     weight_term(2)
     weight_along_x(1)

time: 65.1 us -> 67.4 us (1.035)
  Pallas kernels: 64.1 us -> 66.5 us
    pallas_call x1, Pallas kernels: 61.7 us -> 64.1 us  [body(): pl.pallas_call(functools.partial(kernel, norm), out_shape=shapes, in_spec...]
where the time goes in v4:
time: 67.4 us; the launch traced here: 67.3 us
  Pallas kernels  66.5 us (99%)
  between operations  0.8 us (1%)
    pallas_call x1, Pallas kernels, body(): pl.pallas_call(functools.partial(kernel, norm), out_shape=shapes, in_spec...  64.1 us
    pallas_call x1, Pallas kernels, body(): pl.pallas_call(hand_over, out_shape=shapes, in_specs=[any_spec] * 6, out_...  2.36 us

profile of v4, /device:TPU:1, one launch (start us, length us, event | category | flops | bytes accessed | tf_op | source)
XLA Modules:
  0.0 67.3 jit_solution(9062651587995516734)
XLA Ops:
  0.6 64.1 %block.1 = (bf16[224,1024]{1,0:T(8,128)(2,1)}, bf16[224,1024]{1,0:T(8,128)(2,1)}, bf16[224,1024]{1,0:T(8,128)(2,1)}, bf16[224,1024]{1,0:T(8,128)(2,1)}, f32[9,1024]{1,0:T(8,128)}, /*index=5*/f32[2,1024]{1,0:T(2,128)}) custom-call(bf16[224,1024]{1,0:T(8,128)(2,1)} %bitcast.9, bf16[224,1024]{1,0:T(8,128)(2,1)} %bitcast.10, bf16[224,1024]{1,0:T(8,128)(2,1)} %bitcast.11, ...), custom_call_target="tpu_custom_call" | custom-call | tf_op jit(solution)/shard_map/block/pallas_call | solution.py:532
  64.8 2.4 %hand_over.1 = (bf16[224,1024]{1,0:T(8,128)(2,1)}, bf16[224,1024]{1,0:T(8,128)(2,1)}, bf16[224,1024]{1,0:T(8,128)(2,1)}, bf16[224,1024]{1,0:T(8,128)(2,1)}, f32[9,1024]{1,0:T(8,128)}, /*index=5*/f32[2,1024]{1,0:T(2,128)}) custom-call(bf16[224,1024]{1,0:T(8,128)(2,1)} %get-tuple-element.18.refs_0_, bf16[224,1024]{1,0:T(8,128)(2,1)} %get-tuple-element.19.refs_1_, ...), custom_call_target="tpu_custom_call" | custom-call | tf_op jit(solution)/shard_map/hand_over/pallas_call | solution.py:543
